TPU v7x, 32 devices: a whole 2x2x4 slice. The times are simulated.
32 devices in a mesh: img: 16 (over z, x, core), tok: 2 (over y).
Axes of the slice: x: 2, y: 2, z: 4, core: 2. Of those that a mesh axis runs over, the one named last changes fastest.
Arguments:
- tokens: bfloat16 [16, 2064, 1024], P('img', 'tok'), may hold values from -6 to 6
- block_lengths: int32 [16, 2], P('img'), may hold values from 64 to 1032, as said below
- out_grad: bfloat16 [16, 2064, 1024], P('img', 'tok'), may hold values from -6 to 6
- qkv_weight: float32 [1024, 3072], P(('img', 'tok')), may hold values from -0.1875 to 0.1875
- proj_weight: float32 [1024, 1024], P(('img', 'tok')), may hold values from -3.5 to 3.5
- up_weight: float32 [1024, 4096], P(('img', 'tok')), may hold values from -0.1875 to 0.1875
- down_weight: float32 [4096, 1024], P(('img', 'tok')), may hold values from -0.1875 to 0.1875
- gain_rows: float32 [4, 1024], P(None, ('img', 'tok')), may hold values from 0.25 to 1.75
- bias_rows: float32 [10, 1024], P(None, ('img', 'tok')), may hold values from -3 to 3
- qkv_first: float32 [1024, 3072], P(('img', 'tok')), may hold values from -96 to 96
- proj_first: float32 [1024, 1024], P(('img', 'tok')), may hold values from -5 to 5
- up_first: float32 [1024, 4096], P(('img', 'tok')), may hold values from -96 to 96
- down_first: float32 [4096, 1024], P(('img', 'tok')), may hold values from -56 to 56
- gain_first: float32 [4, 1024], P(None, ('img', 'tok')), may hold values from -192 to 192
- bias_first: float32 [10, 1024], P(None, ('img', 'tok')), may hold values from -96 to 96
- qkv_second: float32 [1024, 3072], P(('img', 'tok')), may hold values from 21.92 to 87.68
- proj_second: float32 [1024, 1024], P(('img', 'tok')), may hold values from 0.0548 to 0.2192
- up_second: float32 [1024, 4096], P(('img', 'tok')), may hold values from 21.92 to 87.68
- down_second: float32 [4096, 1024], P(('img', 'tok')), may hold values from 7.8912 to 31.5648
- gain_second: float32 [4, 1024], P(None, ('img', 'tok')), may hold values from 43.84 to 175.36
- bias_second: float32 [10, 1024], P(None, ('img', 'tok')), may hold values from 21.92 to 87.68
Outputs:
- output: bfloat16 [16, 2064, 1024], P('img', 'tok')
- input_grad: bfloat16 [16, 2064, 1024], P('img', 'tok')
- qkv_first_new: float32 [1024, 3072], P(('img', 'tok'))
- proj_first_new: float32 [1024, 1024], P(('img', 'tok'))
- up_first_new: float32 [1024, 4096], P(('img', 'tok'))
- down_first_new: float32 [4096, 1024], P(('img', 'tok'))
- gain_first_new: float32 [4, 1024], P(None, ('img', 'tok'))
- bias_first_new: float32 [10, 1024], P(None, ('img', 'tok'))
- qkv_second_new: float32 [1024, 3072], P(('img', 'tok'))
- proj_second_new: float32 [1024, 1024], P(('img', 'tok'))
- up_second_new: float32 [1024, 4096], P(('img', 'tok'))
- down_second_new: float32 [4096, 1024], P(('img', 'tok'))
- gain_second_new: float32 [4, 1024], P(None, ('img', 'tok'))
- bias_second_new: float32 [10, 1024], P(None, ('img', 'tok'))
- qkv_new: float32 [1024, 3072], P(('img', 'tok'))
- proj_new: float32 [1024, 1024], P(('img', 'tok'))
- up_new: float32 [1024, 4096], P(('img', 'tok'))
- down_new: float32 [4096, 1024], P(('img', 'tok'))
- gain_new: float32 [4, 1024], P(None, ('img', 'tok'))
- bias_new: float32 [10, 1024], P(None, ('img', 'tok'))
Inputs may be any that keep to these rules, and one draw needn't show every extreme that they name: `block_lengths`: for each image the blocks sum to 1370, each holds 64 or more, and one block of every image holds exactly 1032.
All inputs are finite; a program needn't handle non-finite values.
Results may differ from a plain program's by a relative error of at most 0.013.
The roundings to bfloat16 on the way count: a program that leaves them out, or rounds other values in their place, can miss the bound.
Values may be sent and summed in bfloat16 or wider, within the bound.
A program may use at most 320 MiB of HBM per device.

v0:
```python
from functools import partial

import jax
import jax.numpy as jnp
from jax import lax
from jax.sharding import PartitionSpec as P

HD = 64
STEP = 10


norm_eps = 1e-06
beta_one = 0.9
beta_two = 0.999
adam_eps = 1e-08
learn_rates = (0.1, 1.5, 0.1, 0.05, 0.5, 0.5)
decay_rates = (0.05, 0.05, 0.05, 0.05, 0.0, 0.0)
group_heads = 4


def norm_rows(values, scales, shifts):
    centred = values - jnp.mean(values, axis=-1, keepdims=True)
    spread = jnp.mean(centred * centred, axis=-1, keepdims=True)
    return centred * lax.rsqrt(spread + norm_eps) * scales + shifts


def adam_update(weight, gradient, first, second, rate, decay):
    first_new = beta_one * first + (1.0 - beta_one) * gradient
    second_new = beta_two * second + (1.0 - beta_two) * gradient * gradient
    corrected = first_new / (1.0 - beta_one**STEP)
    scaled = second_new / (1.0 - beta_two**STEP)
    weight_new = weight - rate * (corrected / (jnp.sqrt(scaled) + adam_eps) + decay * weight)
    return (first_new, second_new, weight_new)


def per_device(
    tokens,
    block_lengths,
    out_grad,
    qkv_weight,
    proj_weight,
    up_weight,
    down_weight,
    gain_rows,
    bias_rows,
    qkv_first,
    proj_first,
    up_first,
    down_first,
    gain_first,
    bias_first,
    qkv_second,
    proj_second,
    up_second,
    down_second,
    gain_second,
    bias_second,
):
    gathered = (
        lax.all_gather(qkv_weight.astype(jnp.bfloat16), ("img", "tok"), axis=0, tiled=True),
        lax.all_gather(proj_weight.astype(jnp.bfloat16), ("img", "tok"), axis=0, tiled=True),
        lax.all_gather(up_weight.astype(jnp.bfloat16), ("img", "tok"), axis=0, tiled=True),
        lax.all_gather(down_weight.astype(jnp.bfloat16), ("img", "tok"), axis=0, tiled=True),
        lax.all_gather(gain_rows.astype(jnp.bfloat16), ("img", "tok"), axis=1, tiled=True),
        lax.all_gather(bias_rows.astype(jnp.bfloat16), ("img", "tok"), axis=1, tiled=True),
    )
    w_qkv = gathered[0]
    w_proj = gathered[1]
    w_up = gathered[2]
    w_down = gathered[3]
    gain_all = gathered[4].astype(jnp.float32)
    bias_all = gathered[5].astype(jnp.float32)
    images, capacity, width = tokens.shape
    row_count = images * capacity
    hidden_width = w_up.shape[1]
    tok_count = lax.axis_size("tok")
    tok_here = lax.axis_index("tok")
    key_count = tok_count * capacity
    group_width = group_heads * HD
    group_count = width // group_width
    query_scale = HD ** (-0.5)
    own_length = jnp.sum(
        jnp.where(jnp.arange(tok_count)[None, :] == tok_here, block_lengths, 0), axis=1
    )
    own_valid = jnp.arange(capacity)[None, :] < own_length[:, None]
    row_valid = own_valid.astype(jnp.float32).reshape(row_count, 1)
    key_valid = (jnp.arange(capacity)[None, None, :] < block_lengths[:, :, None]).reshape(
        images, key_count
    )
    values = tokens.reshape(row_count, width).astype(jnp.float32)
    normed = norm_rows(values, gain_all[0], bias_all[0]).astype(jnp.bfloat16)
    mixed_qkv = jnp.dot(normed, w_qkv, preferred_element_type=jnp.float32)
    queries = (
        ((mixed_qkv[:, :width] + bias_all[1]) * query_scale)
        .astype(jnp.bfloat16)
        .reshape(images, capacity, width)
    )
    keyset = mixed_qkv[:, width : 2 * width].astype(jnp.bfloat16).reshape(images, capacity, width)
    valset = (
        (mixed_qkv[:, 2 * width :] + bias_all[2])
        .astype(jnp.bfloat16)
        .reshape(images, capacity, width)
    )
    key_all, value_all = (
        lax.all_gather(keyset, "tok", axis=1, tiled=True),
        lax.all_gather(valset, "tok", axis=1, tiled=True),
    )

    def attend_group(group_index):
        offset = group_index * group_width
        query_part = lax.dynamic_slice_in_dim(queries, offset, group_width, 2).reshape(
            images, capacity, group_heads, HD
        )
        key_part = lax.dynamic_slice_in_dim(key_all, offset, group_width, 2).reshape(
            images, key_count, group_heads, HD
        )
        value_part = lax.dynamic_slice_in_dim(value_all, offset, group_width, 2).reshape(
            images, key_count, group_heads, HD
        )
        scores = jnp.einsum(
            "gqhd,gkhd->ghqk", query_part, key_part, preferred_element_type=jnp.float32
        )
        scores = jnp.where(key_valid[:, None, None, :], scores, -1e30)
        highest = jnp.max(scores, axis=-1, keepdims=True)
        exponent = jnp.exp(scores - highest)
        totals = jnp.sum(exponent, axis=-1, keepdims=True)
        attn_weight = (exponent / totals).astype(jnp.bfloat16)
        out_part = jnp.einsum(
            "ghqk,gkhd->gqhd", attn_weight, value_part, preferred_element_type=jnp.float32
        )
        return (
            out_part.reshape(images, capacity, group_width),
            (highest + jnp.log(totals))[..., 0],
        )

    attended_groups, log_totals = lax.map(attend_group, jnp.arange(group_count))
    attended = attended_groups.transpose(1, 2, 0, 3).reshape(row_count, width).astype(jnp.bfloat16)
    branch = jnp.dot(attended, w_proj, preferred_element_type=jnp.float32) + bias_all[3]
    middle = values + gain_all[1] * branch
    normed_two = norm_rows(middle, gain_all[2], bias_all[4]).astype(jnp.bfloat16)
    hidden_pre = jnp.dot(normed_two, w_up, preferred_element_type=jnp.float32) + bias_all[
        6:
    ].reshape(hidden_width)
    hidden = jax.nn.gelu(hidden_pre, approximate=False).astype(jnp.bfloat16)
    second = jnp.dot(hidden, w_down, preferred_element_type=jnp.float32) + bias_all[5]
    result = middle + gain_all[3] * second
    output = (result * row_valid).reshape(images, capacity, width).astype(jnp.bfloat16)
    grad_out = out_grad.reshape(row_count, width).astype(jnp.float32) * row_valid
    grad_second = (gain_all[3] * grad_out).astype(jnp.bfloat16)
    grad_gain_three = jnp.sum(grad_out * second, axis=0)
    grad_bias_down = jnp.sum(grad_second.astype(jnp.float32), axis=0)
    grad_down = jnp.einsum("rf,rd->fd", hidden, grad_second, preferred_element_type=jnp.float32)
    grad_hidden = jnp.einsum("rd,fd->rf", grad_second, w_down, preferred_element_type=jnp.float32)
    _, gelu_pull = jax.vjp(partial(jax.nn.gelu, approximate=False), hidden_pre)
    grad_hidden_pre = gelu_pull(grad_hidden)[0].astype(jnp.bfloat16)
    grad_bias_up = jnp.sum(grad_hidden_pre.astype(jnp.float32), axis=0).reshape(
        hidden_width // width, width
    )
    grad_up = jnp.einsum(
        "rd,rf->df", normed_two, grad_hidden_pre, preferred_element_type=jnp.float32
    )
    grad_normed_two = jnp.einsum(
        "rf,df->rd", grad_hidden_pre, w_up, preferred_element_type=jnp.float32
    )
    _, norm_two_pull = jax.vjp(norm_rows, middle, gain_all[2], bias_all[4])
    grad_middle_norm, grad_gain_two, grad_shift_two = norm_two_pull(grad_normed_two)
    grad_middle = grad_out + grad_middle_norm
    grad_branch = (gain_all[1] * grad_middle).astype(jnp.bfloat16)
    grad_gain_one = jnp.sum(grad_middle * branch, axis=0)
    grad_bias_proj = jnp.sum(grad_branch.astype(jnp.float32), axis=0)
    grad_proj = jnp.einsum("rd,re->de", attended, grad_branch, preferred_element_type=jnp.float32)
    grad_attended = jnp.einsum("re,de->rd", grad_branch, w_proj, preferred_element_type=jnp.float32)
    grad_attended = grad_attended.astype(jnp.bfloat16).reshape(images, capacity, width)
    key_back, value_back = (key_all, value_all)

    def back_group(inputs):
        group_index, log_part = inputs
        offset = group_index * group_width
        query_part = lax.dynamic_slice_in_dim(queries, offset, group_width, 2).reshape(
            images, capacity, group_heads, HD
        )
        key_part = lax.dynamic_slice_in_dim(key_back, offset, group_width, 2).reshape(
            images, key_count, group_heads, HD
        )
        value_part = lax.dynamic_slice_in_dim(value_back, offset, group_width, 2).reshape(
            images, key_count, group_heads, HD
        )
        grad_part = lax.dynamic_slice_in_dim(grad_attended, offset, group_width, 2).reshape(
            images, capacity, group_heads, HD
        )
        scores = jnp.einsum(
            "gqhd,gkhd->ghqk", query_part, key_part, preferred_element_type=jnp.float32
        )
        scores = jnp.where(key_valid[:, None, None, :], scores, -1e30)
        attn_full = jnp.exp(scores - log_part[..., None])
        grad_attn = jnp.einsum(
            "gqhd,gkhd->ghqk", grad_part, value_part, preferred_element_type=jnp.float32
        )
        inner = jnp.sum(attn_full * grad_attn, axis=-1, keepdims=True)
        grad_scores = (attn_full * (grad_attn - inner)).astype(jnp.bfloat16)
        grad_query = jnp.einsum(
            "ghqk,gkhd->gqhd", grad_scores, key_part, preferred_element_type=jnp.float32
        )
        grad_key = jnp.einsum(
            "ghqk,gqhd->gkhd", grad_scores, query_part, preferred_element_type=jnp.float32
        )
        grad_value = jnp.einsum(
            "ghqk,gqhd->gkhd",
            attn_full.astype(jnp.bfloat16),
            grad_part,
            preferred_element_type=jnp.float32,
        )
        return (
            grad_query.astype(jnp.bfloat16).reshape(images, capacity, group_width),
            grad_key.reshape(images, key_count, group_width),
            grad_value.reshape(images, key_count, group_width),
        )

    grad_query_groups, grad_key_groups, grad_value_groups = lax.map(
        back_group, (jnp.arange(group_count), log_totals)
    )
    grad_query_round = grad_query_groups.transpose(1, 2, 0, 3).reshape(row_count, width)
    grad_key_all = grad_key_groups.transpose(1, 2, 0, 3).reshape(images, key_count, width)
    grad_value_all = grad_value_groups.transpose(1, 2, 0, 3).reshape(images, key_count, width)
    own_key_grad, own_value_grad = (
        lax.psum_scatter(
            grad_key_all.astype(jnp.bfloat16), "tok", scatter_dimension=1, tiled=True
        ).astype(jnp.float32),
        lax.psum_scatter(
            grad_value_all.astype(jnp.bfloat16), "tok", scatter_dimension=1, tiled=True
        ).astype(jnp.float32),
    )
    grad_keys = own_key_grad.reshape(row_count, width).astype(jnp.bfloat16)
    grad_values = own_value_grad.reshape(row_count, width).astype(jnp.bfloat16)
    grad_queries = (grad_query_round.astype(jnp.float32) * query_scale).astype(jnp.bfloat16)
    grad_mixed = jnp.concatenate([grad_queries, grad_keys, grad_values], axis=1)
    grad_bias_query = jnp.sum(grad_queries.astype(jnp.float32), axis=0)
    grad_bias_value = jnp.sum(grad_values.astype(jnp.float32), axis=0)
    grad_qkv = jnp.einsum("rd,re->de", normed, grad_mixed, preferred_element_type=jnp.float32)
    grad_normed = jnp.einsum("re,de->rd", grad_mixed, w_qkv, preferred_element_type=jnp.float32)
    _, norm_one_pull = jax.vjp(norm_rows, values, gain_all[0], bias_all[0])
    grad_values_norm, grad_gain_zero, grad_shift_zero = norm_one_pull(grad_normed)
    input_grad = (
        ((grad_middle + grad_values_norm) * row_valid)
        .reshape(images, capacity, width)
        .astype(jnp.bfloat16)
    )
    grad_gains = jnp.stack([grad_gain_zero, grad_gain_one, grad_gain_two, grad_gain_three])
    grad_biases = jnp.concatenate(
        [
            jnp.stack(
                [
                    grad_shift_zero,
                    grad_bias_query,
                    grad_bias_value,
                    grad_bias_proj,
                    grad_shift_two,
                    grad_bias_down,
                ]
            ),
            grad_bias_up,
        ],
        axis=0,
    )
    summed = (
        lax.psum_scatter(grad_qkv, ("img", "tok"), scatter_dimension=0, tiled=True),
        lax.psum_scatter(grad_proj, ("img", "tok"), scatter_dimension=0, tiled=True),
        lax.psum_scatter(grad_up, ("img", "tok"), scatter_dimension=0, tiled=True),
        lax.psum_scatter(grad_down, ("img", "tok"), scatter_dimension=0, tiled=True),
        lax.psum_scatter(grad_gains, ("img", "tok"), scatter_dimension=1, tiled=True),
        lax.psum_scatter(grad_biases, ("img", "tok"), scatter_dimension=1, tiled=True),
    )
    params = (qkv_weight, proj_weight, up_weight, down_weight, gain_rows, bias_rows)
    firsts = (qkv_first, proj_first, up_first, down_first, gain_first, bias_first)
    seconds = (qkv_second, proj_second, up_second, down_second, gain_second, bias_second)
    updated = [
        adam_update(
            params[position],
            summed[position],
            firsts[position],
            seconds[position],
            learn_rates[position],
            decay_rates[position],
        )
        for position in range(6)
    ]
    return (
        output,
        input_grad,
        updated[0][0],
        updated[1][0],
        updated[2][0],
        updated[3][0],
        updated[4][0],
        updated[5][0],
        updated[0][1],
        updated[1][1],
        updated[2][1],
        updated[3][1],
        updated[4][1],
        updated[5][1],
        updated[0][2],
        updated[1][2],
        updated[2][2],
        updated[3][2],
        updated[4][2],
        updated[5][2],
    )


def solution(mesh):
    return jax.shard_map(
        per_device,
        mesh=mesh,
        in_specs=(
            P("img", "tok", None),
            P("img", None),
            P("img", "tok", None),
            P(("img", "tok"), None),
            P(("img", "tok"), None),
            P(("img", "tok"), None),
            P(("img", "tok"), None),
            P(None, ("img", "tok")),
            P(None, ("img", "tok")),
            P(("img", "tok"), None),
            P(("img", "tok"), None),
            P(("img", "tok"), None),
            P(("img", "tok"), None),
            P(None, ("img", "tok")),
            P(None, ("img", "tok")),
            P(("img", "tok"), None),
            P(("img", "tok"), None),
            P(("img", "tok"), None),
            P(("img", "tok"), None),
            P(None, ("img", "tok")),
            P(None, ("img", "tok")),
        ),
        out_specs=(
            P("img", "tok", None),
            P("img", "tok", None),
            P(("img", "tok"), None),
            P(("img", "tok"), None),
            P(("img", "tok"), None),
            P(("img", "tok"), None),
            P(None, ("img", "tok")),
            P(None, ("img", "tok")),
            P(("img", "tok"), None),
            P(("img", "tok"), None),
            P(("img", "tok"), None),
            P(("img", "tok"), None),
            P(None, ("img", "tok")),
            P(None, ("img", "tok")),
            P(("img", "tok"), None),
            P(("img", "tok"), None),
            P(("img", "tok"), None),
            P(("img", "tok"), None),
            P(None, ("img", "tok")),
            P(None, ("img", "tok")),
        ),
        check_vma=False,
    )
```

profile of v0, /device:TPU:0, one launch (start us, length us, event | category | flops | bytes accessed | tf_op | source)
XLA Modules:
  0.0 2595.5 jit_solution(12508063322587975624)
XLA Ops:
  9.8 70.1 %all-gather.2 = bf16[32,32,4]{1,2,0:T(4,128)(2,1)S(1)} all-gather(bf16[1,32,4]{1,2,0:T(4,128)(2,1)S(1)} %convert_bitcast_fusion.2), channel_id=1, replica_groups=mesh['img'=16,'tok'=2] {'img','tok'}, dimensions={0}, use_global_device_ids=true | all-gather | bytes 8448 | tf_op jit(solution)/shard_map/all_gather | solution.py:64
  80.8 64.0 %all-gather.3 = bf16[32,32,10]{1,2,0:T(8,128)(2,1)S(1)} all-gather(bf16[1,32,10]{1,2,0:T(8,128)(2,1)S(1)} %convert_bitcast_fusion.1), channel_id=1, replica_groups=mesh['img'=16,'tok'=2] {'img','tok'}, dimensions={0}, use_global_device_ids=true | all-gather | bytes 21120 | tf_op jit(solution)/shard_map/all_gather | solution.py:65
  179.4 41.0 %all-gather.21.cloned.1.call-done = bf16[2064,1024]{1,0:T(8,128)(2,1)} async-done(((bf16[1032,1024]{1,0:T(8,128)(2,1)}), bf16[2064,1024]{1,0:T(8,128)(2,1)}) %all-gather.21.cloned.1.call-update) | async-done | bytes 4227088 | tf_op jit(solution)/shard_map/all_gather | solution.py:105
  226.7 52.9 %all-gather.19.cloned.1.call-done = bf16[2064,1024]{1,0:T(8,128)(2,1)} async-done(((bf16[1032,1024]{1,0:T(8,128)(2,1)}), bf16[2064,1024]{1,0:T(8,128)(2,1)}) %all-gather.19.cloned.1.call-update) | async-done | bytes 4227088 | tf_op jit(solution)/shard_map/all_gather | solution.py:106
  286.0 212.1 %while.28 = (s32[]{:T(128)}, bf16[4,1,1032,256]{2,3,1,0:T(8,128)(2,1)}, f32[4,1,4,1032]{3,2,1,0:T(4,128)}, s32[4]{0:T(128)S(1)}, bf16[1,2064,1024]{1,2,0:T(8,128...) while((s32[]{:T(128)}, ...), condition=%wide.region_5.6_spmd.clone, body=%wide.region_2.5_spmd.clone.sunk | while | flops 2240808448 | bytes 112018568 | solution.py:136
  357.1 17.2 fusion.134
  410.2 17.4 fusion.134
  510.1 50.9 %multiply_convert_fusion.1 = (bf16[1032,4096]{1,0:T(8,128)(2,1)S(1)}, f32[1032,4096]{1,0:T(8,128)}, f32[1032,4096]{1,0:T(8,128)}) fusion(f32[4096]{0:T(1024)S(1)} %bitcast.312, bf16[1024,4096]{1,0:T(8,128)(2,1)} %all-gather.15.cloned.1.call-done, f32[1032,1024]{1,0:T(8,128)} %copy-done.4, f32[1024]{0:T(1024)S(1)} %bitcast.314, f32[1024]{0:T(1024)S(1)} %bitcast.299, ...), kind=kOutput, calls=%fused_computation.35 | convolution fusion | flops 8941314048 | bytes 54919232 | tf_op jit(solution)/shard_map/dot_general | solution.py:141
  578.7 357.5 %reduce-scatter.23.cloned.1.call-done = f32[128,1024]{1,0:T(8,128)} async-done(((f32[4096,1024]{1,0:T(8,128)}), f32[128,1024]{1,0:T(8,128)}) %reduce-scatter.23.cloned.1.call-update) | async-done | bytes 524304 | tf_op jit(solution)/shard_map/reduce_scatter | solution.py:269
  939.0 79.4 %all-gather.17.cloned.1.call-done = bf16[4096,1024]{1,0:T(8,128)(2,1)} async-done(((bf16[128,1024]{1,0:T(8,128)(2,1)}), bf16[4096,1024]{1,0:T(8,128)(2,1)}) %all-gather.17.cloned.1.call-update) | async-done | bytes 8388624 | tf_op jit(solution)/shard_map/all_gather | solution.py:63
  1018.4 24.4 convert_reduce_fusion
  1069.9 450.8 %while.29 = (s32[]{:T(128)}, bf16[4,1,1032,256]{2,3,1,0:T(8,128)(2,1)}, bf16[4,1,2064,256]{2,3,1,0:T(8,128)(2,1)}, bf16[4,1,2064,256]{2,3,1,0:T(8,128)(2,1)}, s3...) while((s32[]{:T(128)}, ...), condition=%wide.region_13.14_spmd.clone, body=%wide.region_11.13_spmd.clone.sunk | while | flops 5521346560 | bytes 276479904 | solution.py:219
  1091.8 24.0 multiply_reduce_fusion.6
  1115.8 29.1 %multiply_convert_fusion.8 = bf16[4,1032,2064]{2,1,0:T(8,128)(2,1)} fusion(f32[4,1032,2064]{2,1,0:T(8,128)} %get-tuple-element.478, f32[4,1032,2064]{2,1,0:T(8,128)} %fusion.146, f32[4,1032]{1,0:T(4,128)S(1)} %get-tuple-element.479), kind=kLoop, calls=%fused_computation.16.clone.1 | loop fusion | flops 25560576 | bytes 85218432 | tf_op jit(solution)/shard_map/while/body/eval_jaxpr/convert_element_type | solution.py:200
  1204.5 24.0 multiply_reduce_fusion.6
  1228.5 29.1 %multiply_convert_fusion.8 = bf16[4,1032,2064]{2,1,0:T(8,128)(2,1)} fusion(f32[4,1032,2064]{2,1,0:T(8,128)} %get-tuple-element.478, f32[4,1032,2064]{2,1,0:T(8,128)} %fusion.146, f32[4,1032]{1,0:T(4,128)S(1)} %get-tuple-element.479), kind=kLoop, calls=%fused_computation.16.clone.1 | loop fusion | flops 25560576 | bytes 85218432 | tf_op jit(solution)/shard_map/while/body/eval_jaxpr/convert_element_type | solution.py:200
  1317.0 24.0 multiply_reduce_fusion.6
  1341.0 29.1 %multiply_convert_fusion.8 = bf16[4,1032,2064]{2,1,0:T(8,128)(2,1)} fusion(f32[4,1032,2064]{2,1,0:T(8,128)} %get-tuple-element.478, f32[4,1032,2064]{2,1,0:T(8,128)} %fusion.146, f32[4,1032]{1,0:T(4,128)S(1)} %get-tuple-element.479), kind=kLoop, calls=%fused_computation.16.clone.1 | loop fusion | flops 25560576 | bytes 85218432 | tf_op jit(solution)/shard_map/while/body/eval_jaxpr/convert_element_type | solution.py:200
  1429.6 24.0 multiply_reduce_fusion.6
  1453.6 29.1 %multiply_convert_fusion.8 = bf16[4,1032,2064]{2,1,0:T(8,128)(2,1)} fusion(f32[4,1032,2064]{2,1,0:T(8,128)} %get-tuple-element.478, f32[4,1032,2064]{2,1,0:T(8,128)} %fusion.146, f32[4,1032]{1,0:T(4,128)S(1)} %get-tuple-element.479), kind=kLoop, calls=%fused_computation.16.clone.1 | loop fusion | flops 25560576 | bytes 85218432 | tf_op jit(solution)/shard_map/while/body/eval_jaxpr/convert_element_type | solution.py:200
  1520.8 21.1 copy.75
  1549.0 21.3 copy.77
  1602.4 17.3 reshape_bitcast_fusion.1
  1630.7 28.7 %reduce-scatter.27.cloned.1.call-done = bf16[1032,1024]{1,0:T(8,128)(2,1)} async-done(((bf16[2064,1024]{1,0:T(8,128)(2,1)}), bf16[1032,1024]{1,0:T(8,128)(2,1)}) %reduce-scatter.27.cloned.1.call-update) | async-done | bytes 2113552
  1659.5 17.4 reshape_bitcast_fusion
  1705.1 19.9 convert_reduce_fusion.4
  1745.6 19.3 fusion.65
  1765.1 38.3 %reduce-scatter.19.cloned.1.call-done = f32[32,1024]{1,0:T(8,128)} async-done(((f32[1024,1024]{1,0:T(8,128)}), f32[32,1024]{1,0:T(8,128)}) %reduce-scatter.19.cloned.1.call-update) | async-done | bytes 131088 | tf_op jit(solution)/shard_map/reduce_scatter | solution.py:267
  1805.1 132.2 %reduce-scatter.29.cloned.1.call-done = f32[32,4]{1,0:T(8,128)} async-done(((f32[1024,4]{1,0:T(8,128)}), f32[32,4]{1,0:T(8,128)}) %reduce-scatter.29.cloned.1.call-update) | async-done | bytes 528
  1938.7 131.3 %reduce-scatter.31.cloned.1.call-done = f32[32,10]{1,0:T(8,128)} async-done(((f32[1024,10]{1,0:T(8,128)}), f32[32,10]{1,0:T(8,128)}) %reduce-scatter.31.cloned.1.call-update) | async-done | bytes 1296
  2071.4 155.9 %reduce-scatter.17.cloned.1.call-done = f32[32,3072]{1,0:T(8,128)} async-done(((f32[1024,3072]{1,0:T(8,128)}), f32[32,3072]{1,0:T(8,128)}) %reduce-scatter.17.cloned.1.call-update) | async-done | bytes 393232 | tf_op jit(solution)/shard_map/reduce_scatter | solution.py:266
  2229.5 356.6 %reduce-scatter.21.cloned.1.call-done = f32[32,4096]{1,0:T(8,128)} async-done(((f32[1024,4096]{1,0:T(8,128)}), f32[32,4096]{1,0:T(8,128)}) %reduce-scatter.21.cloned.1.call-update) | async-done | bytes 524304 | tf_op jit(solution)/shard_map/reduce_scatter | solution.py:268
  (340 shorter events, 627.6 us)
Async XLA Ops:
  7.2 141.7 %all-gather.11.cloned.1.call-start = ((), (), s32[]{:S(2)}) async-start(), calls=%async_computation.8 | async-start | bytes 6488064 | tf_op jit(solution)/shard_map/all_gather | solution.py:60
  9.1 211.3 %all-gather.21.cloned.1.call-start = ((), (), s32[]{:S(2)}) async-start(), calls=%async_computation.17 | async-start | bytes 6340608 | tf_op jit(solution)/shard_map/all_gather | solution.py:105
  165.1 114.6 %all-gather.19.cloned.1.call-start = ((), (), s32[]{:S(2)}) async-start(), calls=%async_computation.16 | async-start | bytes 6340608 | tf_op jit(solution)/shard_map/all_gather | solution.py:106
  172.1 326.0 %all-gather.13.cloned.1.call-start = ((), (), s32[]{:S(2)}) async-start(), calls=%async_computation.9 | async-start | bytes 2162688 | tf_op jit(solution)/shard_map/all_gather | solution.py:61
  172.8 337.2 %all-gather.15.cloned.1.call-start = ((), (), s32[]{:S(2)}) async-start(), calls=%async_computation.10 | async-start | bytes 8650752 | tf_op jit(solution)/shard_map/all_gather | solution.py:62
  173.6 762.5 %reduce-scatter.23.cloned.1.call-start = ((), (), s32[]{:S(2)}) async-start(), calls=%async_computation.15 | async-start | bytes 17301504 | tf_op jit(solution)/shard_map/reduce_scatter | solution.py:269
  286.0 212.1 %copy-start.44 = (f32[1,1024]{1,0:T(1,128)S(1)}, f32[1,1024]{1,0:T(1,128)}, u32[]{:S(2)}) copy-start(f32[1,1024]{1,0:T(1,128)} %get-tuple-element.343) | copy-start | bytes 12292
  286.0 212.1 %copy-start.61 = (f32[1,1024]{1,0:T(1,128)S(1)}, f32[1,1024]{1,0:T(1,128)}, u32[]{:S(2)}) copy-start(f32[1,1024]{1,0:T(1,128)} %get-tuple-element.336) | copy-start | bytes 12292
  506.9 552.7 %copy-start.31 = (f32[1032]{0:T(1024)}, f32[1032]{0:T(1024)S(1)}, u32[]{:S(2)}) copy-start(f32[1032]{0:T(1024)S(1)} %broadcast_multiply_fusion) | copy-start | bytes 12388
  510.1 549.5 %copy-start.42 = (f32[1032]{0:T(1024)}, f32[1032]{0:T(1024)S(1)}, u32[]{:S(2)}) copy-start(f32[1032]{0:T(1024)S(1)} %fusion.50) | copy-start | bytes 12388
  578.6 357.5 %copy-start.15 = (f32[128,1024]{1,0:T(8,128)S(1)}, f32[128,1024]{1,0:T(8,128)}, u32[]{:S(2)}) copy-start(f32[128,1024]{1,0:T(8,128)} %param.31) | copy-start | bytes 1572868
  578.6 357.5 %copy-start.16 = (f32[128,1024]{1,0:T(8,128)S(1)}, f32[128,1024]{1,0:T(8,128)}, u32[]{:S(2)}) copy-start(f32[128,1024]{1,0:T(8,128)} %param.43) | copy-start | bytes 1572868
  578.6 439.8 %all-gather.17.cloned.1.call-start = ((), (), s32[]{:S(2)}) async-start(), calls=%async_computation.11 | async-start | bytes 8650752 | tf_op jit(solution)/shard_map/all_gather | solution.py:63
  938.9 663.5 %reduce-scatter.25.cloned.1.call-start = ((), (), s32[]{:S(2)}) async-start(), calls=%async_computation.18 | async-start | bytes 6340608
  1549.0 110.5 %reduce-scatter.27.cloned.1.call-start = ((), (), s32[]{:S(2)}) async-start(), calls=%async_computation.19 | async-start | bytes 6340608
  1577.5 225.8 %reduce-scatter.19.cloned.1.call-start = ((), (), s32[]{:S(2)}) async-start(), calls=%async_computation.13 | async-start | bytes 4325376 | tf_op jit(solution)/shard_map/reduce_scatter | solution.py:267
  1585.4 351.8 %reduce-scatter.29.cloned.1.call-start = ((), (), s32[]{:S(2)}) async-start(), calls=%async_computation.20 | async-start | bytes 540672
  1726.0 344.0 %reduce-scatter.31.cloned.1.call-start = ((), (), s32[]{:S(2)}) async-start(), calls=%async_computation.21 | async-start | bytes 540672
  1729.4 498.0 %reduce-scatter.17.cloned.1.call-start = ((), (), s32[]{:S(2)}) async-start(), calls=%async_computation.12 | async-start | bytes 12976128 | tf_op jit(solution)/shard_map/reduce_scatter | solution.py:266
  1745.0 841.1 %reduce-scatter.21.cloned.1.call-start = ((), (), s32[]{:S(2)}) async-start(), calls=%async_computation.14 | async-start | bytes 17301504 | tf_op jit(solution)/shard_map/reduce_scatter | solution.py:268
  1764.9 173.1 %copy-start.55 = (f32[4,32]{1,0:T(4,128)S(1)}, f32[4,32]{1,0:T(4,128)}, u32[]{:S(2)}) copy-start(f32[4,32]{1,0:T(4,128)} %param.32) | copy-start | bytes 1540
  1764.9 173.1 %copy-start.66 = (f32[4,32]{1,0:T(4,128)S(1)}, f32[4,32]{1,0:T(4,128)}, u32[]{:S(2)}) copy-start(f32[4,32]{1,0:T(4,128)} %param.44) | copy-start | bytes 1540
  1764.9 173.1 %copy-start.67 = (f32[4,32]{1,0:T(4,128)S(1)}, f32[4,32]{1,0:T(4,128)}, u32[]{:S(2)}) copy-start(f32[4,32]{1,0:T(4,128)} %param.38) | copy-start | bytes 1540
  1764.9 305.8 %copy-start.41 = (f32[10,32]{1,0:T(8,128)S(1)}, f32[10,32]{1,0:T(8,128)}, u32[]{:S(2)}) copy-start(f32[10,32]{1,0:T(8,128)} %param.33) | copy-start | bytes 3844
  1765.0 305.8 %copy-start.53 = (f32[10,32]{1,0:T(8,128)S(1)}, f32[10,32]{1,0:T(8,128)}, u32[]{:S(2)}) copy-start(f32[10,32]{1,0:T(8,128)} %param.45) | copy-start | bytes 3844
  1765.0 305.8 %copy-start.54 = (f32[10,32]{1,0:T(8,128)S(1)}, f32[10,32]{1,0:T(8,128)}, u32[]{:S(2)}) copy-start(f32[10,32]{1,0:T(8,128)} %param.39) | copy-start | bytes 3844
  1765.0 462.4 %copy-start.14 = (f32[32,3072]{1,0:T(8,128)S(1)}, f32[32,3072]{1,0:T(8,128)}, u32[]{:S(2)}) copy-start(f32[32,3072]{1,0:T(8,128)} %param.28) | copy-start | bytes 1179652
  1765.0 462.4 %copy-start.21 = (f32[32,3072]{1,0:T(8,128)S(1)}, f32[32,3072]{1,0:T(8,128)}, u32[]{:S(2)}) copy-start(f32[32,3072]{1,0:T(8,128)} %param.40) | copy-start | bytes 1179652
  1765.0 462.4 %copy-start.22 = (f32[32,3072]{1,0:T(8,128)S(1)}, f32[32,3072]{1,0:T(8,128)}, u32[]{:S(2)}) copy-start(f32[32,3072]{1,0:T(8,128)} %param.34) | copy-start | bytes 1179652
  1765.0 821.1 %copy-start.13 = (f32[32,4096]{1,0:T(8,128)S(1)}, f32[32,4096]{1,0:T(8,128)}, u32[]{:S(2)}) copy-start(f32[32,4096]{1,0:T(8,128)} %param.30) | copy-start | bytes 1572868
  1765.0 821.1 %copy-start.17 = (f32[32,4096]{1,0:T(8,128)S(1)}, f32[32,4096]{1,0:T(8,128)}, u32[]{:S(2)}) copy-start(f32[32,4096]{1,0:T(8,128)} %param.42) | copy-start | bytes 1572868
  1765.0 821.1 %copy-start.18 = (f32[32,4096]{1,0:T(8,128)S(1)}, f32[32,4096]{1,0:T(8,128)}, u32[]{:S(2)}) copy-start(f32[32,4096]{1,0:T(8,128)} %param.36) | copy-start | bytes 1572868
  (52 other events, 729.6 us)
Sparse Core Ops, SparseCore 0:
  11.5 72.8 all-gather.10
  165.2 55.1 all-gather.20
  222.5 57.1 all-gather.18
  283.2 56.4 all-gather.12
  343.3 76.2 all-gather.14
  578.8 357.3 reduce-scatter.22
  939.8 78.5 all-gather.16
  1549.1 53.2 reduce-scatter.24
  1604.8 54.6 reduce-scatter.26
  1661.6 141.7 reduce-scatter.18
  1806.2 131.0 reduce-scatter.28
  1940.0 129.9 reduce-scatter.30
  2076.0 151.3 reduce-scatter.16
  2229.6 356.4 reduce-scatter.20
where the time goes:
time: 2610 us; the launch traced here: 2600 us
  waiting for transfers between devices  1390 us (53%)
  matrix products  617 us (24%)
  other arithmetic  227 us (9%)
  local copies, waits for them, and re-layouts  208 us (8%)
  blocking collectives  134 us (5%)
    reduce_scatter x1, waiting for transfers between devices, per_device(): lax.psum_scatter(grad_down, ('img', 'tok'), scatter_dimension=0, tiled=True)  357 us
    reduce_scatter x1, waiting for transfers between devices, per_device(): lax.psum_scatter(grad_up, ('img', 'tok'), scatter_dimension=0, tiled=True)  357 us
    unnamed x18, waiting for transfers between devices  305 us
    reduce_scatter x1, waiting for transfers between devices, per_device(): lax.psum_scatter(grad_qkv, ('img', 'tok'), scatter_dimension=0, tiled=True)  156 us
    unnamed x158, local copies, waits for them, and re-layouts  151 us
    convert_element_type x4, other arithmetic, back_group(): grad_scores = (attn_full * (grad_attn - inner)).astype(jnp.bfloat16)  116 us
    dot_general x4, matrix products, back_group(): jnp.einsum('gqhd,gkhd->ghqk', query_part, key_part, preferred_element_typ...  96 us
    all_gather x1, waiting for transfers between devices, per_device(): lax.all_gather(down_weight.astype(jnp.bfloat16), ('img', 'tok'), axis=0,...  79.4 us
  transfers between devices with their start and end apart: 14, of which 11 were waited for; matrix products, arithmetic and copies ran while one was open for 16% of the time, Pallas kernels for 0%

commit v1 on v0

v1 whole, which is shorter than its diff:
```python
from functools import partial

import jax
import jax.numpy as jnp
from jax import lax
from jax.experimental import pallas as pl
from jax.experimental.pallas import tpu as pltpu
from jax.sharding import PartitionSpec as P

HD = 64
STEP = 10
LEN = 1370
LANES = 128
QUERY_BLOCK = 256
VMEM_BYTES = 28 * 1024 * 1024


norm_eps = 1e-06
beta_one = 0.9
beta_two = 0.999
adam_eps = 1e-08
learn_rates = (0.1, 1.5, 0.1, 0.05, 0.5, 0.5)
decay_rates = (0.05, 0.05, 0.05, 0.05, 0.0, 0.0)


def norm_rows(values, scales, shifts):
    centred = values - jnp.mean(values, axis=-1, keepdims=True)
    spread = jnp.mean(centred * centred, axis=-1, keepdims=True)
    return centred * lax.rsqrt(spread + norm_eps) * scales + shifts


def adam_update(weight, gradient, first, second, rate, decay):
    first_new = beta_one * first + (1.0 - beta_one) * gradient
    second_new = beta_two * second + (1.0 - beta_two) * gradient * gradient
    corrected = first_new / (1.0 - beta_one**STEP)
    scaled = second_new / (1.0 - beta_two**STEP)
    weight_new = weight - rate * (corrected / (jnp.sqrt(scaled) + adam_eps) + decay * weight)
    return (first_new, second_new, weight_new)


def lane_head(shape, head):
    lane = lax.broadcasted_iota(jnp.int32, shape, 1)
    return jnp.logical_and(lane >= head * HD, lane < (head + 1) * HD)


def live_rows(ref, row_count):
    block = ref[...]
    first = pl.program_id(1) * block.shape[0]
    row = first + lax.broadcasted_iota(jnp.int32, block.shape, 0)
    return jnp.where(row < row_count, block, jnp.zeros_like(block))


def scores_by_key(key_pair, query_pair, valid, head):
    query = jnp.where(lane_head(query_pair.shape, head), query_pair, jnp.zeros_like(query_pair))
    scores = lax.dot_general(
        key_pair, query, (((1,), (1,)), ((), ())), preferred_element_type=jnp.float32
    )
    return jnp.where(valid > 0.5, scores, -1e30)


def attend_kernel(row_count, q_ref, k_ref, v_ref, valid_ref, out_ref, log_ref):
    query_pair = live_rows(q_ref, row_count)
    key_pair = k_ref[...]
    value_by_lane = v_ref[...].T
    valid = valid_ref[...]
    parts = []
    for head in range(LANES // HD):
        scores = scores_by_key(key_pair, query_pair, valid, head)
        highest = jnp.max(scores, axis=0, keepdims=True)
        exponent = jnp.exp(scores - highest)
        totals = jnp.sum(exponent, axis=0, keepdims=True)
        attn = (exponent * (1.0 / totals)).astype(jnp.bfloat16)
        parts.append(
            jnp.dot(
                value_by_lane[head * HD : (head + 1) * HD], attn, preferred_element_type=jnp.float32
            )
        )
        log_ref[0, head : head + 1, :] = highest + jnp.log(totals)
    out_ref[...] = jnp.concatenate(parts, axis=0).T.astype(out_ref.dtype)


def back_kernel(
    row_count, q_ref, k_ref, v_ref, g_ref, log_ref, valid_ref, dq_ref, dk_ref, dv_ref
):
    @pl.when(pl.program_id(1) == 0)
    def _():
        dk_ref[...] = jnp.zeros_like(dk_ref)
        dv_ref[...] = jnp.zeros_like(dv_ref)

    query_pair = live_rows(q_ref, row_count)
    grad_pair = live_rows(g_ref, row_count)
    key_pair = k_ref[...]
    value_pair = v_ref[...]
    key_by_lane = key_pair.T
    valid = valid_ref[...]
    parts = []
    for head in range(LANES // HD):
        own = lane_head(query_pair.shape, head)
        query = jnp.where(own, query_pair, jnp.zeros_like(query_pair))
        grad = jnp.where(own, grad_pair, jnp.zeros_like(grad_pair))
        scores = scores_by_key(key_pair, query_pair, valid, head)
        attn = jnp.exp(scores - log_ref[0, head : head + 1, :])
        grad_attn = lax.dot_general(
            value_pair, grad, (((1,), (1,)), ((), ())), preferred_element_type=jnp.float32
        )
        inner = jnp.sum(attn * grad_attn, axis=0, keepdims=True)
        grad_scores = (attn * (grad_attn - inner)).astype(jnp.bfloat16)
        dv_ref[...] += jnp.dot(
            attn.astype(jnp.bfloat16), grad, preferred_element_type=jnp.float32
        )
        dk_ref[...] += jnp.dot(grad_scores, query, preferred_element_type=jnp.float32)
        parts.append(
            jnp.dot(
                key_by_lane[head * HD : (head + 1) * HD],
                grad_scores,
                preferred_element_type=jnp.float32,
            )
        )
    dq_ref[...] = jnp.concatenate(parts, axis=0).T.astype(dq_ref.dtype)


def attention_specs(row_count, key_count, width):
    block = min(QUERY_BLOCK, row_count)
    blocks = -(-row_count // block)
    pairs = width // LANES
    rows = pl.BlockSpec((block, LANES), lambda p, i: (i, p))
    keys = pl.BlockSpec((key_count, LANES), lambda p, i: (0, p))
    logs = pl.BlockSpec((1, LANES // HD, block), lambda p, i: (p, 0, i))
    valid = pl.BlockSpec((key_count, 1), lambda p, i: (0, 0))
    return (block, blocks, pairs, rows, keys, logs, valid)


def attend(queries, keys, values, valid):
    row_count, width = queries.shape
    key_count = keys.shape[0]
    block, blocks, pairs, rows, keyed, logs, valid_spec = attention_specs(
        row_count, key_count, width
    )
    work = row_count * key_count * width
    return pl.pallas_call(
        partial(attend_kernel, row_count),
        grid=(pairs, blocks),
        in_specs=[rows, keyed, keyed, valid_spec],
        out_specs=[rows, logs],
        out_shape=[
            jax.ShapeDtypeStruct((row_count, width), jnp.bfloat16),
            jax.ShapeDtypeStruct((pairs, LANES // HD, blocks * block), jnp.float32),
        ],
        compiler_params=pltpu.CompilerParams(vmem_limit_bytes=VMEM_BYTES),
        cost_estimate=pl.CostEstimate(
            flops=16 * work, bytes_accessed=4 * key_count * width, transcendentals=work // HD
        ),
        name="attend",
    )(queries, keys, values, valid)


def attend_back(queries, keys, values, grads, logs_in, valid):
    row_count, width = queries.shape
    key_count = keys.shape[0]
    block, blocks, pairs, rows, keyed, logs, valid_spec = attention_specs(
        row_count, key_count, width
    )
    work = row_count * key_count * width
    return pl.pallas_call(
        partial(back_kernel, row_count),
        grid=(pairs, blocks),
        in_specs=[rows, keyed, keyed, rows, logs, valid_spec],
        out_specs=[rows, keyed, keyed],
        out_shape=[
            jax.ShapeDtypeStruct((row_count, width), jnp.bfloat16),
            jax.ShapeDtypeStruct((key_count, width), jnp.float32),
            jax.ShapeDtypeStruct((key_count, width), jnp.float32),
        ],
        compiler_params=pltpu.CompilerParams(vmem_limit_bytes=VMEM_BYTES),
        cost_estimate=pl.CostEstimate(
            flops=40 * work, bytes_accessed=12 * key_count * width, transcendentals=work // HD
        ),
        name="attend_back",
    )(queries, keys, values, grads, logs_in, valid)


def reduce_rows(gradient):
    return lax.psum_scatter(
        gradient, ("img", "tok"), scatter_dimension=0, tiled=True
    ).astype(jnp.float32)


def per_device(
    tokens,
    block_lengths,
    out_grad,
    qkv_weight,
    proj_weight,
    up_weight,
    down_weight,
    gain_rows,
    bias_rows,
    qkv_first,
    proj_first,
    up_first,
    down_first,
    gain_first,
    bias_first,
    qkv_second,
    proj_second,
    up_second,
    down_second,
    gain_second,
    bias_second,
):
    capacity, width = tokens.shape[1:]
    tok_count = lax.axis_size("tok")
    tok_here = lax.axis_index("tok")
    w_qkv = lax.all_gather(qkv_weight.astype(jnp.bfloat16), ("img", "tok"), axis=0, tiled=True)
    rows_all = lax.all_gather(
        jnp.concatenate([gain_rows, bias_rows], axis=0).astype(jnp.bfloat16),
        ("img", "tok"),
        axis=1,
        tiled=True,
    ).astype(jnp.float32)
    w_proj = lax.all_gather(proj_weight.astype(jnp.bfloat16), ("img", "tok"), axis=0, tiled=True)
    w_up = lax.all_gather(up_weight.astype(jnp.bfloat16), ("img", "tok"), axis=0, tiled=True)
    w_down = lax.all_gather(down_weight.astype(jnp.bfloat16), ("img", "tok"), axis=0, tiled=True)
    gain_count = gain_rows.shape[0]
    gain_all = rows_all[:gain_count]
    bias_all = rows_all[gain_count:]
    hidden_width = w_up.shape[1]
    query_scale = HD ** (-0.5)
    lengths = block_lengths[0]
    own_length = lengths[tok_here]
    short = -(-(LEN - capacity) // 8) * 8
    balanced = tok_count == 2 and capacity > short and (capacity - short) % 16 == 0
    swap = [(0, 1), (1, 0)]
    is_full = own_length > short
    if balanced:
        row_count = (capacity + short) // 2
        moved = row_count - short

        def take_rows(block):
            received = lax.ppermute(block[row_count:], "tok", swap)
            kept = jnp.where(is_full, block[short:row_count], received)
            return jnp.concatenate([block[:short], kept], axis=0)

        def give_rows(block):
            received = lax.ppermute(block[short:], "tok", swap)
            kept = jnp.where(is_full, block[short:], 0)
            tail = jnp.where(is_full, received, 0)
            return jnp.concatenate([block[:short], kept, tail], axis=0)

        def live_of(length):
            row = jnp.arange(row_count)
            return jnp.logical_or(row < length, row >= short)

    else:
        row_count = capacity

        def take_rows(block):
            return block

        def give_rows(block):
            return block

        def live_of(length):
            return jnp.arange(row_count) < length

    row_valid = live_of(own_length).astype(jnp.float32)[:, None]
    if tok_count == 2:
        key_valid = jnp.concatenate([live_of(own_length), live_of(lengths[1 - tok_here])])

        def gather_rows(block):
            return jnp.concatenate([block, lax.ppermute(block, "tok", swap)], axis=0)

        def scatter_rows(block):
            received = lax.ppermute(block[row_count:].astype(jnp.bfloat16), "tok", swap)
            return (block[:row_count] + received.astype(jnp.float32)).astype(jnp.bfloat16)

    else:
        key_valid = jnp.concatenate([live_of(lengths[place]) for place in range(tok_count)])

        def gather_rows(block):
            return lax.all_gather(block, "tok", axis=0, tiled=True)

        def scatter_rows(block):
            return lax.psum_scatter(
                block.astype(jnp.bfloat16), "tok", scatter_dimension=0, tiled=True
            )

    key_valid = key_valid.astype(jnp.float32)[:, None]
    values = take_rows(tokens[0]).astype(jnp.float32)
    normed = norm_rows(values, gain_all[0], bias_all[0]).astype(jnp.bfloat16)
    keyset = jnp.dot(
        normed, w_qkv[:, width : 2 * width], preferred_element_type=jnp.float32
    ).astype(jnp.bfloat16)
    valset = (
        jnp.dot(normed, w_qkv[:, 2 * width :], preferred_element_type=jnp.float32) + bias_all[2]
    ).astype(jnp.bfloat16)
    key_all = gather_rows(keyset)
    value_all = gather_rows(valset)
    queries = (
        (jnp.dot(normed, w_qkv[:, :width], preferred_element_type=jnp.float32) + bias_all[1])
        * query_scale
    ).astype(jnp.bfloat16)
    attended, log_totals = attend(queries, key_all, value_all, key_valid)
    branch = jnp.dot(attended, w_proj, preferred_element_type=jnp.float32) + bias_all[3]
    middle = values + gain_all[1] * branch
    normed_two = norm_rows(middle, gain_all[2], bias_all[4]).astype(jnp.bfloat16)
    hidden_pre = jnp.dot(normed_two, w_up, preferred_element_type=jnp.float32) + bias_all[
        6:
    ].reshape(hidden_width)
    hidden = jax.nn.gelu(hidden_pre, approximate=False).astype(jnp.bfloat16)
    second = jnp.dot(hidden, w_down, preferred_element_type=jnp.float32) + bias_all[5]
    result = middle + gain_all[3] * second
    output = give_rows((result * row_valid).astype(jnp.bfloat16))[None]
    grad_out = take_rows(out_grad[0]).astype(jnp.float32) * row_valid
    grad_second = (gain_all[3] * grad_out).astype(jnp.bfloat16)
    grad_gain_three = jnp.sum(grad_out * second, axis=0)
    grad_bias_down = jnp.sum(grad_second.astype(jnp.float32), axis=0)
    grad_down = jnp.einsum(
        "rf,rd->fd", hidden, grad_second, preferred_element_type=jnp.float32
    ).astype(jnp.bfloat16)
    grad_down, w_down = lax.optimization_barrier((grad_down, w_down))
    sum_down = reduce_rows(grad_down)
    grad_hidden = jnp.einsum("rd,fd->rf", grad_second, w_down, preferred_element_type=jnp.float32)
    _, gelu_pull = jax.vjp(partial(jax.nn.gelu, approximate=False), hidden_pre)
    grad_hidden_pre = gelu_pull(grad_hidden)[0].astype(jnp.bfloat16)
    grad_bias_up = jnp.sum(grad_hidden_pre.astype(jnp.float32), axis=0).reshape(
        hidden_width // width, width
    )
    grad_up = jnp.einsum(
        "rd,rf->df", normed_two, grad_hidden_pre, preferred_element_type=jnp.float32
    ).astype(jnp.bfloat16)
    grad_up, grad_hidden_pre = lax.optimization_barrier((grad_up, grad_hidden_pre))
    grad_normed_two = jnp.einsum(
        "rf,df->rd", grad_hidden_pre, w_up, preferred_element_type=jnp.float32
    )
    _, norm_two_pull = jax.vjp(norm_rows, middle, gain_all[2], bias_all[4])
    grad_middle_norm, grad_gain_two, grad_shift_two = norm_two_pull(grad_normed_two)
    grad_middle = grad_out + grad_middle_norm
    grad_branch = (gain_all[1] * grad_middle).astype(jnp.bfloat16)
    grad_gain_one = jnp.sum(grad_middle * branch, axis=0)
    grad_bias_proj = jnp.sum(grad_branch.astype(jnp.float32), axis=0)
    grad_proj = jnp.einsum(
        "rd,re->de", attended, grad_branch, preferred_element_type=jnp.float32
    ).astype(jnp.bfloat16)
    grad_proj, grad_branch = lax.optimization_barrier((grad_proj, grad_branch))
    grad_attended = jnp.einsum("re,de->rd", grad_branch, w_proj, preferred_element_type=jnp.float32)
    grad_attended = grad_attended.astype(jnp.bfloat16)
    grad_attended, sum_down, grad_up = lax.optimization_barrier((grad_attended, sum_down, grad_up))
    sum_up = reduce_rows(grad_up)
    grad_query_round, grad_key_all, grad_value_all = attend_back(
        queries, key_all, value_all, grad_attended, log_totals, key_valid
    )
    grad_key_all, grad_value_all, sum_up, grad_proj = lax.optimization_barrier(
        (grad_key_all, grad_value_all, sum_up, grad_proj)
    )
    sum_proj = reduce_rows(grad_proj)
    grad_keys = scatter_rows(grad_key_all)
    grad_values = scatter_rows(grad_value_all)
    grad_queries = (grad_query_round.astype(jnp.float32) * query_scale).astype(jnp.bfloat16)
    grad_mixed = jnp.concatenate([grad_queries, grad_keys, grad_values], axis=1)
    grad_bias_query = jnp.sum(grad_queries.astype(jnp.float32), axis=0)
    grad_bias_value = jnp.sum(grad_values.astype(jnp.float32), axis=0)
    grad_qkv = jnp.einsum(
        "rd,re->de", normed, grad_mixed, preferred_element_type=jnp.float32
    ).astype(jnp.bfloat16)
    grad_qkv, grad_mixed, sum_proj = lax.optimization_barrier((grad_qkv, grad_mixed, sum_proj))
    sum_qkv = reduce_rows(grad_qkv)
    grad_normed = jnp.einsum("re,de->rd", grad_mixed, w_qkv, preferred_element_type=jnp.float32)
    _, norm_one_pull = jax.vjp(norm_rows, values, gain_all[0], bias_all[0])
    grad_values_norm, grad_gain_zero, grad_shift_zero = norm_one_pull(grad_normed)
    input_grad = (
        give_rows(((grad_middle + grad_values_norm) * row_valid).astype(jnp.bfloat16))[None]
    )
    grad_gains = jnp.stack([grad_gain_zero, grad_gain_one, grad_gain_two, grad_gain_three])
    grad_biases = jnp.concatenate(
        [
            jnp.stack(
                [
                    grad_shift_zero,
                    grad_bias_query,
                    grad_bias_value,
                    grad_bias_proj,
                    grad_shift_two,
                    grad_bias_down,
                ]
            ),
            grad_bias_up,
        ],
        axis=0,
    )
    grad_rows, sum_qkv = lax.optimization_barrier(
        (jnp.concatenate([grad_gains, grad_biases], axis=0), sum_qkv)
    )
    small = lax.psum_scatter(
        grad_rows,
        ("img", "tok"),
        scatter_dimension=1,
        tiled=True,
    )
    summed = (
        sum_qkv,
        sum_proj,
        sum_up,
        sum_down,
        small[:gain_count],
        small[gain_count:],
    )
    params = (qkv_weight, proj_weight, up_weight, down_weight, gain_rows, bias_rows)
    firsts = (qkv_first, proj_first, up_first, down_first, gain_first, bias_first)
    seconds = (qkv_second, proj_second, up_second, down_second, gain_second, bias_second)
    updated = [
        adam_update(
            params[position],
            summed[position],
            firsts[position],
            seconds[position],
            learn_rates[position],
            decay_rates[position],
        )
        for position in range(6)
    ]
    return (
        output,
        input_grad,
        updated[0][0],
        updated[1][0],
        updated[2][0],
        updated[3][0],
        updated[4][0],
        updated[5][0],
        updated[0][1],
        updated[1][1],
        updated[2][1],
        updated[3][1],
        updated[4][1],
        updated[5][1],
        updated[0][2],
        updated[1][2],
        updated[2][2],
        updated[3][2],
        updated[4][2],
        updated[5][2],
    )


def solution(mesh):
    return jax.shard_map(
        per_device,
        mesh=mesh,
        in_specs=(
            P("img", "tok", None),
            P("img", None),
            P("img", "tok", None),
            P(("img", "tok"), None),
            P(("img", "tok"), None),
            P(("img", "tok"), None),
            P(("img", "tok"), None),
            P(None, ("img", "tok")),
            P(None, ("img", "tok")),
            P(("img", "tok"), None),
            P(("img", "tok"), None),
            P(("img", "tok"), None),
            P(("img", "tok"), None),
            P(None, ("img", "tok")),
            P(None, ("img", "tok")),
            P(("img", "tok"), None),
            P(("img", "tok"), None),
            P(("img", "tok"), None),
            P(("img", "tok"), None),
            P(None, ("img", "tok")),
            P(None, ("img", "tok")),
        ),
        out_specs=(
            P("img", "tok", None),
            P("img", "tok", None),
            P(("img", "tok"), None),
            P(("img", "tok"), None),
            P(("img", "tok"), None),
            P(("img", "tok"), None),
            P(None, ("img", "tok")),
            P(None, ("img", "tok")),
            P(("img", "tok"), None),
            P(("img", "tok"), None),
            P(("img", "tok"), None),
            P(("img", "tok"), None),
            P(None, ("img", "tok")),
            P(None, ("img", "tok")),
            P(("img", "tok"), None),
            P(("img", "tok"), None),
            P(("img", "tok"), None),
            P(("img", "tok"), None),
            P(None, ("img", "tok")),
            P(None, ("img", "tok")),
        ),
        check_vma=False,
    )
```

time: 2610 us -> 1090 us (0.42)
  waiting for transfers between devices: 1390 us -> 619 us
  matrix products: 617 us -> 141 us
  other arithmetic: 227 us -> 42.5 us
  local copies, waits for them, and re-layouts: 208 us -> 36.9 us
  Pallas kernels: 0 us -> 131 us
  blocking collectives: 134 us -> 92.4 us
    reduce_scatter x4, waiting for transfers between devices: 908 us -> 320 us  [reduce_rows(): lax.psum_scatter(gradient, ('img', 'tok'), scatter_dimension=0, tiled=True)]
    dot_general x29 -> x3, matrix products: 425 us -> 11.1 us  [the longest x1 4.36 us: per_device(): jnp.dot(normed, w_qkv[:, width:2 * width], preferred_element_type=jnp.flo...]
    unnamed x18 -> x10, waiting for transfers between devices: 305 us -> 132 us
    ppermute x0 -> x8, waiting for transfers between devices: none -> 166 us  [the longest x2 85.2 us: scatter_rows(): received = lax.ppermute(block[row_count:].astype(jnp.bfloat16), 'tok', swap)]
    pallas_call x0 -> x2, Pallas kernels: none -> 131 us  [the longest x1 69.3 us: attend_back(): pl.pallas_call(partial(back_kernel, row_count), grid=(pairs, blocks), in_...]
    unnamed x158 -> x171, local copies, waits for them, and re-layouts: 151 us -> 26.5 us
    convert_element_type x8 -> x10, other arithmetic: 120 us -> 9.76 us  [the longest x4 5.23 us: reduce_rows(): return lax.psum_scatter(gradient, ('img', 'tok'), scatter_dimension=0, ti...]
    all_gather x2 -> x0, waiting for transfers between devices: 94 us -> none  [the longest x1 52.9 us: per_device(): lax.all_gather(valset, 'tok', axis=1, tiled=True)]
  transfers between devices with their start and end apart: 14 -> 17, of which waited for: 11 -> 11; matrix products, arithmetic and copies ran while one was open for 16% -> 17% of each run, Pallas kernels for 0% -> 12%
where the time goes in v1:
time: 1090 us
  waiting for transfers between devices  619 us (57%)
  matrix products  141 us (13%)
  Pallas kernels  131 us (12%)
  blocking collectives  92.4 us (8%)
  other arithmetic  42.5 us (4%)
  local copies, waits for them, and re-layouts  36.9 us (3%)
  between operations  15.8 us (1%)
    reduce_scatter x4, waiting for transfers between devices, reduce_rows(): lax.psum_scatter(gradient, ('img', 'tok'), scatter_dimension=0, tiled=True)  320 us
    unnamed x10, waiting for transfers between devices  132 us
    all_gather x1, blocking collectives, per_device(): lax.all_gather(jnp.concatenate([gain_rows, bias_rows], axis=0).astype(jnp...  92.4 us
    ppermute x2, waiting for transfers between devices, scatter_rows(): received = lax.ppermute(block[row_count:].astype(jnp.bfloat16), 'tok', swap)  85.2 us
    pallas_call x1, Pallas kernels, attend_back(): pl.pallas_call(partial(back_kernel, row_count), grid=(pairs, blocks), in_...  69.3 us
    pallas_call x1, Pallas kernels, attend(): pl.pallas_call(partial(attend_kernel, row_count), grid=(pairs, blocks), i...  61.3 us
    ppermute x2, waiting for transfers between devices, gather_rows(): return jnp.concatenate([block, lax.ppermute(block, 'tok', swap)], axis=0)  56 us
    dot_general x1, matrix products, per_device(): jnp.dot(normed_two, w_up, preferred_element_type=jnp.float32)  35.3 us
  transfers between devices with their start and end apart: 17, of which 11 were waited for; matrix products, arithmetic and copies ran while one was open for 17% of the time, Pallas kernels for 12%

profile of v1, /device:TPU:0, one launch (start us, length us, event | category | flops | bytes accessed | tf_op | source)
XLA Modules:
  0.0 1086.2 jit_solution(3202073256860415555)
XLA Ops:
  15.0 3.0 collective-permute-start
  22.8 92.4 %all-gather = bf16[32,32,14]{1,2,0:T(8,128)(2,1)S(1)} all-gather(bf16[1,32,14]{1,2,0:T(8,128)(2,1)S(1)} %maximum_bitcast_fusion.2), channel_id=1, replica_groups=mesh['img'=16,'tok'=2] {'img','tok'}, dimensions={0}, use_global_device_ids=true | all-gather | bytes 29568 | tf_op jit(solution)/shard_map/all_gather | solution.py:215
  118.9 4.4 fusion.23
  123.3 3.3 add_convert_fusion.4
  131.5 3.5 multiply_convert_fusion.6.q_ref
  135.0 26.1 %collective-permute-done.1 = bf16[688,1024]{1,0:T(8,128)(2,1)} collective-permute-done((bf16[688,1024]{1,0:T(8,128)(2,1)}, bf16[688,1024]{1,0:T(8,128)(2,1)}, u32[]{:S(2)}, u32[]{:S(2)}) %collective-permute-start.1) | collective-permute-done | bytes 1409056 | tf_op jit(solution)/shard_map/ppermute | solution.py:271
  163.2 29.9 %collective-permute-done.2 = bf16[688,1024]{1,0:T(8,128)(2,1)} collective-permute-done((bf16[688,1024]{1,0:T(8,128)(2,1)S(1)}, bf16[688,1024]{1,0:T(8,128)(2,1)}, u32[]{:S(2)}, u32[]{:S(2)}) %collective-permute-start.2) | collective-permute-done | bytes 1409056 | tf_op jit(solution)/shard_map/ppermute | solution.py:271
  194.7 61.3 %attend.1 = (bf16[688,1024]{1,0:T(8,128)(2,1)S(1)}, f32[8,2,768]{2,1,0:T(2,128)S(1)}) custom-call(bf16[688,1024]{1,0:T(8,128)(2,1)S(1)} %multiply_convert_fusion.6.q_ref, bf16[1376,1024]{1,0:T(8,128)(2,1)S(1)} %pad_maximum_fusion.1.k_ref, bf16[1376,1024]{1,0:T(8,128)(2,1)S(1)} %pad_maximum_fusion.2.v_ref, f32[1376,1]{1,0:T(8,128)S(1)} %convert_element_type.146.valid_ref), custom_call_target="tpu_custom_call" | custom-call | flops 15510536192 | bytes 5636096 | tf_op jit(solution)/shard_map/attend/pallas_call | solution.py:140
  258.2 5.5 fusion.57
  265.7 35.3 %multiply_convert_fusion = (bf16[688,4096]{1,0:T(8,128)(2,1)S(1)}, f32[688,4096]{1,0:T(8,128)}, f32[688,4096]{1,0:T(8,128)}) fusion(f32[4096]{0:T(1024)S(1)} %bitcast.92, bf16[1024,4096]{1,0:T(8,128)(2,1)} %all-gather.10.cloned.1.call-done, f32[688,1024]{1,0:T(8,128)} %copy-done.24, f32[1024]{0:T(1024)S(1)} %bitcast.112, f32[1024]{0:T(1024)S(1)} %bitcast.85, ...), kind=kOutput, calls=%fused_computation.4 | convolution fusion | flops 5960876032 | bytes 39417216 | tf_op jit(solution)/shard_map/dot_general | solution.py:307
  303.5 9.5 convolution_convert_fusion.1
  313.1 20.1 %convert_reduce_fusion = (f32[4096]{0:T(1024)}, bf16[688,4096]{1,0:T(8,128)(2,1)}) fusion(f32[688,4096]{1,0:T(8,128)} %get-tuple-element.101, bf16[4096,1024]{1,0:T(8,128)(2,1)} %all-gather.12.cloned.1.call-done, f32[688]{0:T(1024)S(1)} %fusion.40, f32[1024]{0:T(1024)S(1)} %bitcast.105, bf16[344,1024]{1,0:T(8,128)(2,1)S(1)} %bitcast_select_fusion, ...), kind=kOutput, calls=%fused_computation.2 | convolution fusion | flops 5824196608 | bytes 38017728 | tf_op jit(solution)/shard_map/rd,fd->rf/dot_general | solution.py:323
  333.2 11.9 %convolution_convert_fusion = bf16[1024,4096]{1,0:T(8,128)(2,1)} fusion(bf16[688,4096]{1,0:T(8,128)(2,1)} %get-tuple-element.45, f32[688,1024]{1,0:T(8,128)S(1)} %copy-done.25, f32[1024]{0:T(1024)S(1)} %bitcast.113, f32[1024]{0:T(1024)S(1)} %bitcast.86, f32[688]{0:T(1024)S(1)} %fusion.38, f32[688]{0:T(1024)S(1)} %broadcast_multiply_fusion), kind=kOutput, calls=%fused_computation.18 | convolution fusion | flops 5779079168 | bytes 16856448 | tf_op jit(solution)/shard_map/rd,rf->df/dot_general | solution.py:329
  345.1 10.9 %multiply_reduce_fusion.1 = (f32[1024]{0:T(1024)S(1)}, f32[688]{0:T(1024)S(1)}, f32[1024]{0:T(1024)S(1)}, f32[688,1024]{1,0:T(8,128)S(1)}) fusion(f32[688,1024]{1,0:T(8,128)S(1)} %copy-done.25, f32[688]{0:T(1024)S(1)} %fusion.38, f32[688]{0:T(1024)S(1)} %broadcast_multiply_fusion, f32[1024]{0:T(1024)S(1)} %bitcast.87, ...), kind=kOutput, calls=%fused_computation.47 | convolution fusion | flops 5776995840 | bytes 19681344 | tf_op jit(solution)/shard_map/rf,df->rd/dot_general | solution.py:333
  358.4 14.0 %convert_reduce_fusion.2 = (f32[1024]{0:T(1024)S(1)}, f32[1024]{0:T(1024)S(1)}, f32[1024]{0:T(1024)}, f32[1024]{0:T(1024)}, bf16[688,1024]{1,0:T(8,128)(2,1)S(1)}, /*index=5*/bf16[688,1024]{1,0:T(8,128)(2,1)}) fusion(f32[688]{0:T(1024)S(1)} %fusion.40, bf16[344,1024]{1,0:T(8,128)(2,1)S(1)} %bitcast_select_fusion, bf16[344,1024]{1,0:T(8,128)(2,1)S(1)} %copy-done.29, ...), kind=kOutput, calls=%fused_computation.42 | convolution fusion | flops 5788971008 | bytes 26744192 | tf_op jit(solution)/shard_map/dot_general | solution.py:311
  373.4 3.2 convolution_convert_fusion.3
  376.6 4.2 convolution_convert_fusion.4.g_ref
  380.8 113.5 %reduce-scatter.8.cloned.1.call-done = bf16[128,1024]{1,0:T(8,128)(2,1)} async-done(((bf16[4096,1024]{1,0:T(8,128)(2,1)}), bf16[128,1024]{1,0:T(8,128)(2,1)}) %reduce-scatter.8.cloned.1.call-update) | async-done | bytes 262160 | tf_op jit(solution)/shard_map/reduce_scatter | solution.py:183
  503.4 69.3 %attend_back.1 = (bf16[688,1024]{1,0:T(8,128)(2,1)S(1)}, f32[1376,1024]{1,0:T(8,128)S(1)}, f32[1376,1024]{1,0:T(8,128)S(1)}) custom-call(bf16[688,1024]{1,0:T(8,128)(2,1)S(1)} %copy-done.15, bf16[1376,1024]{1,0:T(8,128)(2,1)S(1)} %copy-done.4, bf16[1376,1024]{1,0:T(8,128)(2,1)S(1)} %copy-done.6, bf16[688,1024]{1,0:T(8,128)(2,1)S(1)} %copy-done.13, ...), custom_call_target="tpu_custom_call" | custom-call | flops 38776340480 | bytes 16908288 | tf_op jit(solution)/shard_map/attend_back/pallas_call | solution.py:164
  572.7 2.5 copy-done
  578.7 101.4 %reduce-scatter.10.cloned.1.call-done = bf16[32,4096]{1,0:T(8,128)(2,1)} async-done(((bf16[1024,4096]{1,0:T(8,128)(2,1)}), bf16[32,4096]{1,0:T(8,128)(2,1)}) %reduce-scatter.10.cloned.1.call-update) | async-done | bytes 262160 | tf_op jit(solution)/shard_map/reduce_scatter | solution.py:183
  688.0 42.7 %collective-permute-done.6 = bf16[688,1024]{1,0:T(8,128)(2,1)S(1)} collective-permute-done((bf16[688,1024]{1,0:T(8,128)(2,1)S(1)}, bf16[688,1024]{1,0:T(8,128)(2,1)S(1)}, u32[]{:S(2)}, u32[]{:S(2)}) %collective-permute-start.6) | collective-permute-done | bytes 1409056 | tf_op jit(solution)/shard_map/ppermute | solution.py:274
  731.3 42.5 %collective-permute-done.5 = bf16[688,1024]{1,0:T(8,128)(2,1)S(1)} collective-permute-done((bf16[688,1024]{1,0:T(8,128)(2,1)S(1)}, bf16[688,1024]{1,0:T(8,128)(2,1)S(1)}, u32[]{:S(2)}, u32[]{:S(2)}) %collective-permute-start.5) | collective-permute-done | bytes 1409056 | tf_op jit(solution)/shard_map/ppermute | solution.py:274
  774.4 2.4 pad_maximum_fusion
  776.9 8.1 convolution_convert_fusion.2
  784.9 37.3 %reduce-scatter.12.cloned.1.call-done = bf16[32,1024]{1,0:T(8,128)(2,1)} async-done(((bf16[1024,1024]{1,0:T(8,128)(2,1)}), bf16[32,1024]{1,0:T(8,128)(2,1)}) %reduce-scatter.12.cloned.1.call-update) | async-done | bytes 65552 | tf_op jit(solution)/shard_map/reduce_scatter | solution.py:183
  826.2 15.4 %collective-permute-done.3 = bf16[344,1024]{1,0:T(8,128)(2,1)} collective-permute-done((bf16[344,1024]{1,0:T(8,128)(2,1)}, bf16[344,1024]{1,0:T(8,128)(2,1)}, u32[]{:S(2)}, u32[]{:S(2)}) %collective-permute-start.3) | collective-permute-done | bytes 704544 | tf_op jit(solution)/shard_map/ppermute | solution.py:245
  845.2 7.1 fusion.48
  854.7 2.5 multiply_convert_fusion.1
  862.0 9.7 collective-permute-done.7
  873.3 67.6 %reduce-scatter.14.cloned.1.call-done = bf16[32,3072]{1,0:T(8,128)(2,1)} async-done(((bf16[1024,3072]{1,0:T(8,128)(2,1)}), bf16[32,3072]{1,0:T(8,128)(2,1)}) %reduce-scatter.14.cloned.1.call-update) | async-done | bytes 196624 | tf_op jit(solution)/shard_map/reduce_scatter | solution.py:183
  944.2 132.3 %reduce-scatter.16.cloned.1.call-done = f32[32,14]{1,0:T(8,128)} async-done(((f32[1024,14]{1,0:T(8,128)}), f32[32,14]{1,0:T(8,128)}) %reduce-scatter.16.cloned.1.call-update) | async-done | bytes 1808
  (265 shorter events, 77.9 us)
Async XLA Ops:
  7.2 111.7 %all-gather.6.cloned.1.call-start = ((), (), s32[]{:S(2)}) async-start(), calls=%async_computation.5 | async-start | bytes 6488064 | tf_op jit(solution)/shard_map/all_gather | solution.py:214
  9.1 249.0 %all-gather.8.cloned.1.call-start = ((), (), s32[]{:S(2)}) async-start(), calls=%async_computation.6 | async-start | bytes 2162688 | tf_op jit(solution)/shard_map/all_gather | solution.py:221
  10.7 255.0 %all-gather.10.cloned.1.call-start = ((), (), s32[]{:S(2)}) async-start(), calls=%async_computation.7 | async-start | bytes 8650752 | tf_op jit(solution)/shard_map/all_gather | solution.py:222
  12.6 300.3 %all-gather.12.cloned.1.call-start = ((), (), s32[]{:S(2)}) async-start(), calls=%async_computation.8 | async-start | bytes 8650752 | tf_op jit(solution)/shard_map/all_gather | solution.py:223
  15.0 243.2 %copy-start.20 = (bf16[344,1024]{1,0:T(8,128)(2,1)}, bf16[344,1024]{1,0:T(8,128)(2,1)S(1)}, u32[]{:S(2)}) copy-start(bf16[344,1024]{1,0:T(8,128)(2,1)S(1)} %get-tuple-element.109) | copy-start | bytes 2113540
  15.0 101.7 %collective-permute-start = (bf16[344,1024]{1,0:T(8,128)(2,1)}, bf16[344,1024]{1,0:T(8,128)(2,1)}, u32[]{:S(2)}, u32[]{:S(2)}) collective-permute-start(bf16[344,1024]{1,0:T(8,128)(2,1)} %get-tuple-element.110), channel_id=1, source_target_pairs={{0,1},{1,0},{2,3},{3,2},{4,5},{5,4},{6,7},{7,6},{8,9},{9,8},{10,11... | collective-permute-start | bytes 2113544 | tf_op jit(solution)/shard_map/ppermute | solution.py:240
  19.2 110.7 %collective-permute-start.4 = (bf16[344,1024]{1,0:T(8,128)(2,1)}, bf16[344,1024]{1,0:T(8,128)(2,1)}, u32[]{:S(2)}, u32[]{:S(2)}) collective-permute-start(bf16[344,1024]{1,0:T(8,128)(2,1)} %get-tuple-element.108), channel_id=1, source_target_pairs={{0,1},{1,0},{2,3},{3,2},{4,5},{5,4},{6,7},{7,6},{8,9},{9,8},{10,11... | collective-permute-start | bytes 2113544 | tf_op jit(solution)/shard_map/ppermute | solution.py:240
  20.1 474.3 %reduce-scatter.8.cloned.1.call-start = ((), (), s32[]{:S(2)}) async-start(), calls=%async_computation.9 | async-start | bytes 8650752 | tf_op jit(solution)/shard_map/reduce_scatter | solution.py:183
  116.6 141.5 %copy-start.67 = (f32[1,1024]{1,0:T(1,128)}, f32[1,1024]{1,0:T(1,128)S(1)}, u32[]{:S(2)}) copy-start(f32[1,1024]{1,0:T(1,128)S(1)} %get-tuple-element.123) | copy-start | bytes 12292
  116.6 196.4 %copy-start.64 = (f32[1,1024]{1,0:T(1,128)}, f32[1,1024]{1,0:T(1,128)S(1)}, u32[]{:S(2)}) copy-start(f32[1,1024]{1,0:T(1,128)S(1)} %get-tuple-element.119) | copy-start | bytes 12292
  118.1 140.1 %copy-start.18 = (bf16[344,1024]{1,0:T(8,128)(2,1)}, bf16[344,1024]{1,0:T(8,128)(2,1)S(1)}, u32[]{:S(2)}) copy-start(bf16[344,1024]{1,0:T(8,128)(2,1)S(1)} %bitcast_select_fusion.1) | copy-start | bytes 2113540
  123.3 37.8 %collective-permute-start.1 = (bf16[688,1024]{1,0:T(8,128)(2,1)}, bf16[688,1024]{1,0:T(8,128)(2,1)}, u32[]{:S(2)}, u32[]{:S(2)}) collective-permute-start(bf16[688,1024]{1,0:T(8,128)(2,1)} %fusion.23), channel_id=1, source_target_pairs={{0,1},{1,0},{2,3},{3,2},{4,5},{5,4},{6,7},{7,6},{8,9},{9,8},{10,11... | collective-permute-start | bytes 4227080 | tf_op jit(solution)/shard_map/ppermute | solution.py:271
  126.6 66.5 %collective-permute-start.2 = (bf16[688,1024]{1,0:T(8,128)(2,1)S(1)}, bf16[688,1024]{1,0:T(8,128)(2,1)}, u32[]{:S(2)}, u32[]{:S(2)}) collective-permute-start(bf16[688,1024]{1,0:T(8,128)(2,1)S(1)} %add_convert_fusion.4), channel_id=1, source_target_pairs={{0,1},{1,0},{2,3},{3,2},{4,5},{5,4},{6,7},{7,6},{8,9},{9,8},{10,11... | collective-permute-start | bytes 4227080 | tf_op jit(solution)/shard_map/ppermute | solution.py:271
  131.5 225.5 %copy-start.26 = (bf16[344,1024]{1,0:T(8,128)(2,1)}, bf16[344,1024]{1,0:T(8,128)(2,1)S(1)}, u32[]{:S(2)}) copy-start(bf16[344,1024]{1,0:T(8,128)(2,1)S(1)} %bitcast_select_fusion) | copy-start | bytes 2113540
  313.0 367.0 %reduce-scatter.10.cloned.1.call-start = ((), (), s32[]{:S(2)}) async-start(), calls=%async_computation.10 | async-start | bytes 8650752 | tf_op jit(solution)/shard_map/reduce_scatter | solution.py:183
  496.1 326.1 %reduce-scatter.12.cloned.1.call-start = ((), (), s32[]{:S(2)}) async-start(), calls=%async_computation.11 | async-start | bytes 2162688 | tf_op jit(solution)/shard_map/reduce_scatter | solution.py:183
  681.1 259.9 %reduce-scatter.14.cloned.1.call-start = ((), (), s32[]{:S(2)}) async-start(), calls=%async_computation.12 | async-start | bytes 6488064 | tf_op jit(solution)/shard_map/reduce_scatter | solution.py:183
  683.2 47.5 %collective-permute-start.6 = (bf16[688,1024]{1,0:T(8,128)(2,1)S(1)}, bf16[688,1024]{1,0:T(8,128)(2,1)S(1)}, u32[]{:S(2)}, u32[]{:S(2)}) collective-permute-start(bf16[688,1024]{1,0:T(8,128)(2,1)S(1)} %slice.212), channel_id=1, source_target_pairs={{0,1},{1,0},{2,3},{3,2},{4,5},{5,4},{6,7},{7,6},{8,9},{9,8},{10,11... | collective-permute-start | bytes 4227080 | tf_op jit(solution)/shard_map/ppermute | solution.py:274
  683.3 90.5 %slice-start = ((s8[5636096]{0:T(1024)(128)(4,1)}), s8[4194304]{0:T(1024)(128)(4,1)S(1)}, s32[]{:S(2)}) async-start(s8[5636096]{0:T(1024)(128)(4,1)} %bitcast.69), calls=%async_computation.14 | async-start | bytes 8388608
  685.5 88.3 %collective-permute-start.5 = (bf16[688,1024]{1,0:T(8,128)(2,1)S(1)}, bf16[688,1024]{1,0:T(8,128)(2,1)S(1)}, u32[]{:S(2)}, u32[]{:S(2)}) collective-permute-start(bf16[688,1024]{1,0:T(8,128)(2,1)S(1)} %slice.213), channel_id=1, source_target_pairs={{0,1},{1,0},{2,3},{3,2},{4,5},{5,4},{6,7},{7,6},{8,9},{9,8},{10,11... | collective-permute-start | bytes 4227080 | tf_op jit(solution)/shard_map/ppermute | solution.py:274
  687.5 86.2 %slice-start.1 = ((s8[5636096]{0:T(1024)(128)(4,1)}), s8[1441792]{0:T(1024)(128)(4,1)S(1)}, s32[]{:S(2)}) async-start(s8[5636096]{0:T(1024)(128)(4,1)} %bitcast.69), calls=%async_computation.15 | async-start | bytes 2883584
  823.8 252.7 %reduce-scatter.16.cloned.1.call-start = ((), (), s32[]{:S(2)}) async-start(), calls=%async_computation.13 | async-start | bytes 540672
  826.1 15.5 %collective-permute-start.3 = (bf16[344,1024]{1,0:T(8,128)(2,1)}, bf16[344,1024]{1,0:T(8,128)(2,1)}, u32[]{:S(2)}, u32[]{:S(2)}) collective-permute-start(bf16[344,1024]{1,0:T(8,128)(2,1)} %get-tuple-element.118), channel_id=1, source_target_pairs={{0,1},{1,0},{2,3},{3,2},{4,5},{5,4},{6,7},{7,6},{8,9},{9,8},{10,11... | collective-permute-start | bytes 2113544 | tf_op jit(solution)/shard_map/ppermute | solution.py:245
  857.4 14.3 %collective-permute-start.7 = (bf16[344,1024]{1,0:T(8,128)(2,1)S(1)}, bf16[344,1024]{1,0:T(8,128)(2,1)S(1)}, u32[]{:S(2)}, u32[]{:S(2)}) collective-permute-start(bf16[344,1024]{1,0:T(8,128)(2,1)S(1)} %get-tuple-element.115), channel_id=1, source_target_pairs={{0,1},{1,0},{2,3},{3,2},{4,5},{5,4},{6,7},{7,6},{8,9},{9,8},{10,11... | collective-permute-start | bytes 2113544 | tf_op jit(solution)/shard_map/ppermute | solution.py:245
  871.8 71.2 %copy-start.36 = (f32[32,3072]{1,0:T(8,128)S(1)}, f32[32,3072]{1,0:T(8,128)}, u32[]{:S(2)}) copy-start(f32[32,3072]{1,0:T(8,128)} %param.24) | copy-start | bytes 1179652
  871.8 71.2 %copy-start.42 = (f32[32,3072]{1,0:T(8,128)S(1)}, f32[32,3072]{1,0:T(8,128)}, u32[]{:S(2)}) copy-start(f32[32,3072]{1,0:T(8,128)} %param.36) | copy-start | bytes 1179652
  873.3 204.9 %copy-start.59 = (f32[4,32]{1,0:T(4,128)S(1)}, f32[4,32]{1,0:T(4,128)}, u32[]{:S(2)}) copy-start(f32[4,32]{1,0:T(4,128)} %param.28) | copy-start | bytes 1540
  873.3 204.9 %copy-start.72 = (f32[4,32]{1,0:T(4,128)S(1)}, f32[4,32]{1,0:T(4,128)}, u32[]{:S(2)}) copy-start(f32[4,32]{1,0:T(4,128)} %param.40) | copy-start | bytes 1540
  873.3 204.9 %copy-start.73 = (f32[4,32]{1,0:T(4,128)S(1)}, f32[4,32]{1,0:T(4,128)}, u32[]{:S(2)}) copy-start(f32[4,32]{1,0:T(4,128)} %param.34) | copy-start | bytes 1540
  873.3 205.5 %copy-start.53 = (f32[10,32]{1,0:T(8,128)S(1)}, f32[10,32]{1,0:T(8,128)}, u32[]{:S(2)}) copy-start(f32[10,32]{1,0:T(8,128)} %param.29) | copy-start | bytes 3844
  873.3 205.5 %copy-start.56 = (f32[10,32]{1,0:T(8,128)S(1)}, f32[10,32]{1,0:T(8,128)}, u32[]{:S(2)}) copy-start(f32[10,32]{1,0:T(8,128)} %param.41) | copy-start | bytes 3844
  873.3 205.5 %copy-start.57 = (f32[10,32]{1,0:T(8,128)S(1)}, f32[10,32]{1,0:T(8,128)}, u32[]{:S(2)}) copy-start(f32[10,32]{1,0:T(8,128)} %param.35) | copy-start | bytes 3844
  (68 other events, 697.3 us)
Sparse Core Ops, SparseCore 0:
  11.5 75.3 all-gather.5
  90.6 57.6 all-gather.7
  151.9 79.1 all-gather.9
  234.6 75.8 all-gather.11
  313.1 181.1 reduce-scatter.7
  496.5 183.5 reduce-scatter.9
  682.9 139.3 reduce-scatter.11
  828.8 112.0 reduce-scatter.13
  943.1 133.2 reduce-scatter.15
